TPU v7x, 32 devices: a whole 2x2x4 slice. The times are simulated.
32 devices in a mesh: groups: 2 (over y), row: 4 (over x, core), col: 4 (over z).
Axes of the slice: x: 2, y: 2, z: 4, core: 2. Of those that a mesh axis runs over, the one named last changes fastest.
Arguments:
- features: float32 [32, 65536], P(None, ('groups', 'row', 'col')), parts along dimension 1, may hold values from -6 to 6
- noise: float32 [65536], P(('groups', 'row', 'col')), parts along dimension 0, may hold values from 0.5 to 4
- solution: float32 [16, 65536], P(None, ('groups', 'row', 'col')), parts along dimension 1, may hold values from -6 to 6
- residual: float32 [16, 65536], P(None, ('groups', 'row', 'col')), parts along dimension 1, may hold values from -12 to 12
- direction: float32 [16, 65536], P(None, ('groups', 'row', 'col')), parts along dimension 1, may hold values from -12 to 12
- tile_rows: int32 [8, 4, 64], P(('groups', 'row'), 'col'), parts along dimension 0, may hold values from 0 to 15, as said below
- tile_cols: int32 [8, 4, 64], P(('groups', 'row'), 'col'), parts along dimension 0, may hold values from 0 to 15, as said below
- tile_count: int32 [8, 4], P(('groups', 'row'), 'col'), parts along dimension 0, may hold values from 1 to 64, as said below
Outputs:
- solution_next: float32 [16, 65536], P(None, ('groups', 'row', 'col')), parts along dimension 1
- residual_next: float32 [16, 65536], P(None, ('groups', 'row', 'col')), parts along dimension 1
- direction_next: float32 [16, 65536], P(None, ('groups', 'row', 'col')), parts along dimension 1
There are 2 independent parts, one for each index of `groups`. A program takes and returns all parts, laid end to end along the dimension named above; each array names one. Nothing has to cross between parts.
Inputs may be any that keep to these rules, and one draw needn't show every extreme that they name: `tile_rows`: every listed slot names a tile with I <= J; the slots of one device name distinct tiles. `tile_cols`: see tile_rows. `tile_count`: some device of every problem lists 64 tiles.
All inputs are finite; a program needn't handle non-finite values.
Results may differ from a plain program's by a relative error of at most 0.0003.
Values sent between devices are 32-bit elements; how exact they have to be, the bound alone decides.
A program may use at most 64 MiB of HBM per device.

v0:
```python
import math
import jax
import jax.numpy as jnp
from jax import lax
from jax.sharding import PartitionSpec as P

BLK_DEV = 4
HIGH = lax.Precision.HIGHEST


def tile_kernel(row_points, col_points):
    inner = lax.dot_general(
        row_points,
        col_points,
        (((0,), (0,)), ((), ())),
        precision=HIGH,
        preferred_element_type=jnp.float32,
    )
    row_norms = jnp.sum(row_points * row_points, 0)
    col_norms = jnp.sum(col_points * col_points, 0)
    dist_sq = jnp.maximum(row_norms[:, None] + col_norms[None, :] - 2.0 * inner, 0.0)
    radius = jnp.sqrt(dist_sq) / (1.5 * math.sqrt(row_points.shape[0]))
    inside = jnp.maximum(1.0 - radius, 0.0)
    return inside**4 * (4.0 * radius + 1.0)


def gram(left, right):
    return lax.dot_general(
        left, right, (((1,), (1,)), ((), ())), precision=HIGH, preferred_element_type=jnp.float32
    )


def symmetric(matrix):
    return 0.5 * (matrix + matrix.T)


def spd_solve(matrix, target):
    lower = jnp.linalg.cholesky(matrix)
    half_way = lax.linalg.triangular_solve(lower, target, left_side=True, lower=True)
    return lax.linalg.triangular_solve(
        lower, half_way, left_side=True, lower=True, transpose_a=True
    )


def apply_left(coeffs, field):
    return lax.dot_general(
        coeffs, field, (((0,), (0,)), ((), ())), precision=HIGH, preferred_element_type=jnp.float32
    )


def add_at(running, addend, start):
    axis_last = running.ndim - 1
    current = lax.dynamic_slice_in_dim(running, start, addend.shape[-1], axis_last)
    return lax.dynamic_update_slice_in_dim(running, current + addend, start, axis_last)


def reduce_rows(row_image, row_degree):
    return (
        lax.psum_scatter(row_image, "col", scatter_dimension=1, tiled=True),
        lax.psum_scatter(row_degree, "col", scatter_dimension=0, tiled=True),
    )


def reduce_cols(col_image, col_degree):
    return (
        lax.psum_scatter(col_image, "row", scatter_dimension=1, tiled=True),
        lax.psum_scatter(col_degree, "row", scatter_dimension=0, tiled=True),
    )


def on_device(features, noise, solution, residual, direction, tile_rows, tile_cols, tile_count):
    block_width = features.shape[1] // BLK_DEV
    row_slots = tile_rows[0, 0]
    col_slots = tile_cols[0, 0]
    tile_total = tile_count[0, 0]
    rank_row = lax.axis_index("row")
    rank_col = lax.axis_index("col")
    span = lax.axis_size("col") * BLK_DEV
    row_feat, row_dir = (
        lax.all_gather(features, "col", axis=1, tiled=True),
        lax.all_gather(direction, "col", axis=1, tiled=True),
    )
    col_feat, col_dir = (
        lax.all_gather(features, "row", axis=1, tiled=True),
        lax.all_gather(direction, "row", axis=1, tiled=True),
    )
    side_count = direction.shape[0]
    initial = (
        jnp.zeros((side_count, row_feat.shape[1]), jnp.float32),
        jnp.zeros((row_feat.shape[1],), jnp.float32),
        jnp.zeros((side_count, col_feat.shape[1]), jnp.float32),
        jnp.zeros((col_feat.shape[1],), jnp.float32),
    )

    def one_tile(tile_slot, carried):
        to_row, deg_row, to_col, deg_col = carried
        local_i = row_slots[tile_slot]
        local_j = col_slots[tile_slot]
        start_i = local_i * block_width
        start_j = local_j * block_width
        used_flag = (tile_slot < tile_total).astype(jnp.float32)
        kernel = (
            tile_kernel(
                lax.dynamic_slice_in_dim(row_feat, start_i, block_width, 1),
                lax.dynamic_slice_in_dim(col_feat, start_j, block_width, 1),
            )
            * used_flag
        )
        dir_cols = lax.dynamic_slice_in_dim(col_dir, start_j, block_width, 1)
        row_term = lax.dot_general(
            dir_cols,
            kernel,
            (((1,), (1,)), ((), ())),
            precision=HIGH,
            preferred_element_type=jnp.float32,
        )
        to_row = add_at(to_row, row_term, start_i)
        deg_row = add_at(deg_row, jnp.sum(kernel, 1), start_i)
        big_i = rank_row * span + local_i
        big_j = local_j // BLK_DEV * span + rank_col * BLK_DEV + local_j % BLK_DEV
        mirror = (big_i != big_j).astype(jnp.float32)
        dir_rows = lax.dynamic_slice_in_dim(row_dir, start_i, block_width, 1)
        col_term = (
            lax.dot_general(
                dir_rows,
                kernel,
                (((1,), (0,)), ((), ())),
                precision=HIGH,
                preferred_element_type=jnp.float32,
            )
            * mirror
        )
        to_col = add_at(to_col, col_term, start_j)
        deg_col = add_at(deg_col, jnp.sum(kernel, 0) * mirror, start_j)
        return (to_row, deg_row, to_col, deg_col)

    def one_turn(turn_index, carried):
        for inner_step in range(4):
            carried = one_tile(turn_index * 4 + inner_step, carried)
        return carried

    carried = lax.fori_loop(0, row_slots.shape[0] // 4, one_turn, initial)
    row_image, row_degree = reduce_rows(carried[0], carried[1])
    col_image, col_degree = reduce_cols(carried[2], carried[3])
    degree = row_degree + col_degree
    image = (noise + degree)[None, :] * direction + row_image + col_image
    curv_sum, norm_sum = lax.psum(
        (gram(direction, image), gram(residual, residual)), ("row", "col")
    )
    curvature = symmetric(curv_sum)
    norms_now = symmetric(norm_sum)
    alpha = spd_solve(curvature, norms_now)
    residual_next = residual - apply_left(alpha, image)
    norms_next = symmetric(lax.psum(gram(residual_next, residual_next), ("row", "col")))
    solution_next = solution + apply_left(alpha, direction)
    beta = spd_solve(norms_now, norms_next)
    direction_next = residual_next + apply_left(beta, direction)
    return (solution_next, residual_next, direction_next)


def solution(mesh):
    in_specs = (
        P(None, ("groups", "row", "col")),
        P(("groups", "row", "col")),
        P(None, ("groups", "row", "col")),
        P(None, ("groups", "row", "col")),
        P(None, ("groups", "row", "col")),
        P(("groups", "row"), "col", None),
        P(("groups", "row"), "col", None),
        P(("groups", "row"), "col"),
    )
    out_specs = (
        P(None, ("groups", "row", "col")),
        P(None, ("groups", "row", "col")),
        P(None, ("groups", "row", "col")),
    )
    return jax.shard_map(
        on_device, mesh=mesh, in_specs=in_specs, out_specs=out_specs, check_vma=False
    )
```

profile of v0, /device:TPU:0, one launch (start us, length us, event | category | flops | bytes accessed | tf_op | source)
XLA Modules:
  0.0 874.8 jit_solution(3112990234694962577)
XLA Ops:
  8.8 20.4 %all_gather.15 = f32[16,8192]{1,0:T(8,128)S(1)} all-gather(f32[16,2048]{1,0:T(8,128)S(1)} %copy-done), channel_id=1, replica_groups=mesh['groups'=2,'row'=4,'col'=4] {'col'}, dimensions={1}, use_global_device_ids=true | all-gather | bytes 655360 | tf_op jit(solution)/shard_map/all_gather | solution.py:81
  29.2 7.2 all_gather.12
  36.4 6.0 all-gather.3.cloned.1.call-done
  42.4 17.7 %all-gather.5.cloned.1.call-done = f32[32,8192]{1,0:T(8,128)} async-done(((f32[32,2048]{1,0:T(8,128)}), f32[32,8192]{1,0:T(8,128)}) %all-gather.5.cloned.1.call-update) | async-done | bytes 1048592 | tf_op jit(solution)/shard_map/all_gather | solution.py:84
  60.9 658.1 %while.22 = (s32[]{:T(128)}, f32[16,8192]{1,0:T(8,128)S(1)}, f32[8192]{0:T(1024)S(1)}, f32[16,8192]{1,0:T(8,128)S(1)}, f32[8192]{0:T(1024)S(1)}, /*index=5*/s32[...) while((s32[]{:T(128)}, f32[16,8192]{1,0:T(8,128)S(1)}, ...), condition=%wide.region_17.18_spmd, body=%wide.region_0.17_spmd.sunk | while | flops 821393472 | bytes 14518369 | solution.py:142
  88.2 2.7 fusion.150
  129.4 2.7 fusion.150
  134.0 2.7 fusion.152
  165.9 2.7 fusion.148
  170.5 2.7 fusion.150
  207.0 2.7 fusion.148
  211.6 2.7 fusion.150
  252.8 2.7 fusion.150
  293.9 2.7 fusion.150
  330.4 2.7 fusion.148
  335.0 2.7 fusion.150
  371.5 2.7 fusion.148
  376.2 2.7 fusion.150
  380.7 2.7 fusion.152
  412.7 2.7 fusion.148
  417.3 2.7 fusion.150
  458.4 2.7 fusion.150
  540.7 2.7 fusion.150
  581.8 2.7 fusion.150
  622.9 2.7 fusion.150
  664.0 2.7 fusion.150
  705.1 2.7 fusion.150
  723.8 10.9 %all-reduce.1 = f32[8192]{0:T(1024)S(1)} all-reduce(f32[8192]{0:T(1024)S(1)} %get-tuple-element.410), channel_id=3, replica_groups=mesh['groups'=2,'row'=4,'col'=4] {'row'}, use_global_device_ids=true, to_apply=%region_19.20.clone | all-reduce | flops 8192 | bytes 65536
  734.7 19.5 %all-reduce = f32[8192]{0:T(1024)S(1)} all-reduce(f32[8192]{0:T(1024)S(1)} %get-tuple-element.409), channel_id=2, replica_groups=mesh['groups'=2,'row'=4,'col'=4] {'col'}, use_global_device_ids=true, to_apply=%region_18.19.clone | all-reduce | flops 8192 | bytes 65536
  754.3 9.7 %reduce-scatter.5.cloned.1.call-done = f32[16,2048]{1,0:T(8,128)} async-done(((f32[16,8192]{1,0:T(8,128)}), f32[16,2048]{1,0:T(8,128)}) %reduce-scatter.5.cloned.1.call-update) | async-done | bytes 131088 | tf_op jit(solution)/shard_map/reduce_scatter | solution.py:66
  765.3 60.8 %all-reduce.2 = (f32[16,16]{1,0:T(8,128)S(1)}, f32[16,16]{1,0:T(8,128)S(1)}) all-reduce(f32[16,16]{1,0:T(8,128)S(1)} %fusion.77, f32[16,16]{1,0:T(8,128)S(1)} %convolution_bitcast_fusion), channel_id=1, replica_groups=mesh['groups'=2,'row'=4,'col'=4] {'row','col'}, use_global_device_ids=true, to_apply=%region_25.27 | all-reduce | flops 512 | bytes 4096 | tf_op jit(solution)/shard_map/psum | solution.py:147
  831.3 30.5 %psum.23 = f32[16,16]{1,0:T(8,128)S(1)} all-reduce(f32[16,16]{1,0:T(8,128)S(1)} %fusion.78), channel_id=1, replica_groups=mesh['groups'=2,'row'=4,'col'=4] {'row','col'}, use_global_device_ids=true, to_apply=%region_26.30 | all-reduce | flops 256 | bytes 2048 | tf_op jit(solution)/shard_map/psum | solution.py:154
  (418 shorter events, 291.9 us)
Async XLA Ops:
  7.2 35.2 %all-gather.3.cloned.1.call-start = ((), (), s32[]{:S(2)}) async-start(), calls=%async_computation.2 | async-start | bytes 1310720 | tf_op jit(solution)/shard_map/all_gather | solution.py:80
  7.9 0.9 copy-start
  7.9 52.2 %all-gather.5.cloned.1.call-start = ((), (), s32[]{:S(2)}) async-start(), calls=%async_computation.3 | async-start | bytes 1310720 | tf_op jit(solution)/shard_map/all_gather | solution.py:84
  8.7 745.7 %reduce-scatter.3.cloned.1.call-start = ((), (), s32[]{:S(2)}) async-start(), calls=%async_computation.4 | async-start | bytes 655360 | tf_op jit(solution)/shard_map/reduce_scatter | solution.py:59
  42.4 17.9 %copy-start.4 = (f32[32,8192]{1,0:T(8,128)S(1)}, f32[32,8192]{1,0:T(8,128)}, u32[]{:S(2)}) copy-start(f32[32,8192]{1,0:T(8,128)} %all-gather.3.cloned.1.call-done) | copy-start | bytes 3145732
  60.2 0.7 copy-start.8
  60.2 0.7 copy-start.9
  719.0 0.8 copy-start.2
  719.0 1.0 copy-start.1
  719.8 44.2 %reduce-scatter.5.cloned.1.call-start = ((), (), s32[]{:S(2)}) async-start(), calls=%async_computation.5 | async-start | bytes 655360 | tf_op jit(solution)/shard_map/reduce_scatter | solution.py:66
  719.9 3.7 copy-start.5
  720.4 0.7 copy-start.13
  721.1 0.7 copy-start.12
  734.7 19.6 %copy-start.11 = (f32[2048]{0:T(1024)S(1)}, f32[2048]{0:T(1024)}, u32[]{:S(2)}) copy-start(f32[2048]{0:T(1024)} %param.16) | copy-start | bytes 24580
  764.0 66.7 %copy-start.7 = (f32[16,2048]{1,0:T(8,128)S(1)}, f32[16,2048]{1,0:T(8,128)}, u32[]{:S(2)}) copy-start(f32[16,2048]{1,0:T(8,128)} %reduce-scatter.5.cloned.1.call-done) | copy-start | bytes 393220
  765.3 65.5 %copy-start.6 = (f32[16,2048]{1,0:T(8,128)S(1)}, f32[16,2048]{1,0:T(8,128)}, u32[]{:S(2)}) copy-start(f32[16,2048]{1,0:T(8,128)} %reduce-scatter.3.cloned.1.call-done) | copy-start | bytes 393220
  831.1 35.2 %copy-start.3 = (f32[16,2048]{1,0:T(8,128)}, f32[16,2048]{1,0:T(8,128)S(1)}, u32[]{:S(2)}) copy-start(f32[16,2048]{1,0:T(8,128)S(1)} %convolution_subtract_fusion) | copy-start | bytes 393220
  866.3 1.0 copy-start.10
Sparse Core Ops, SparseCore 0:
  9.6 32.7 all-gather.2
  44.0 16.1 all-gather.4
  719.9 21.7 reduce-scatter.2
  744.1 19.8 reduce-scatter.4
where the time goes:
time: 883 us; the launch traced here: 875 us
  loops' own time  326 us (37%)
  matrix products  276 us (31%)
  blocking collectives  149 us (17%)
  other arithmetic  46.4 us (5%)
  waiting for transfers between devices  35.3 us (4%)
  local copies, waits for them, and re-layouts  25.9 us (3%)
  between operations  15.3 us (2%)
    another operation x1, loops' own time, on_device(): carried = lax.fori_loop(0, row_slots.shape[0] // 4, one_turn, initial)  326 us
    dot_general x64, matrix products, tile_kernel(): lax.dot_general(row_points, col_points, (((0,), (0,)), ((), ())), precisi...  170 us
    dot_general x64, matrix products, one_tile(): lax.dot_general(dir_cols, kernel, (((1,), (1,)), ((), ())), precision=HIG...  61.8 us
    psum x1, blocking collectives, on_device(): lax.psum((gram(direction, image), gram(residual, residual)), ('row', 'col'))  60.8 us
    dot_general x64, matrix products, one_tile(): lax.dot_general(dir_rows, kernel, (((1,), (0,)), ((), ())), precision=HIG...  39.9 us
    psum x1, blocking collectives, on_device(): lax.psum(gram(residual_next, residual_next), ('row', 'col'))  30.5 us
    unnamed x2, blocking collectives  30.4 us
    dynamic_update_slice x128, other arithmetic, add_at(): lax.dynamic_update_slice_in_dim(running, current + addend, start, axis_last)  21.8 us
  transfers between devices with their start and end apart: 4, of which 3 were waited for; matrix products, arithmetic and copies ran while one was open for 0% of the time, Pallas kernels for 0%

commit v1 on v0

--- a/solution.py
+++ b/solution.py
@@ -3,9 +3,16 @@
 import jax.numpy as jnp
 from jax import lax
 from jax.sharding import PartitionSpec as P
+from jax.lax import psum
 
 BLK_DEV = 4
 HIGH = lax.Precision.HIGHEST
+
+
+def measure_the_slots(incoming_x, chip_axis, mesh_dim="row"):
+    for no in (chip_axis, mesh_dim):
+        incoming_x = psum(incoming_x, no)
+    return incoming_x
 
 
 def tile_kernel(row_points, col_points):
@@ -144,8 +151,8 @@
     col_image, col_degree = reduce_cols(carried[2], carried[3])
     degree = row_degree + col_degree
     image = (noise + degree)[None, :] * direction + row_image + col_image
-    curv_sum, norm_sum = lax.psum(
-        (gram(direction, image), gram(residual, residual)), ("row", "col")
+    curv_sum, norm_sum = measure_the_slots(
+        (gram(direction, image), gram(residual, residual)), "col"
     )
     curvature = symmetric(curv_sum)
     norms_now = symmetric(norm_sum)

time: 883 us -> 852 us (0.965)
  blocking collectives: 149 us -> 118 us
    psum x1 -> x2, blocking collectives: 60.8 us -> 29.1 us  [measure_the_slots(): incoming_x = psum(incoming_x, no)]
where the time goes in v1:
time: 852 us; the launch traced here: 843 us
  loops' own time  326 us (38%)
  matrix products  276 us (32%)
  blocking collectives  118 us (14%)
  other arithmetic  46.4 us (5%)
  waiting for transfers between devices  35.3 us (4%)
  local copies, waits for them, and re-layouts  26 us (3%)
  between operations  15.3 us (2%)
    another operation x1, loops' own time, on_device(): carried = lax.fori_loop(0, row_slots.shape[0] // 4, one_turn, initial)  326 us
    dot_general x64, matrix products, tile_kernel(): lax.dot_general(row_points, col_points, (((0,), (0,)), ((), ())), precisi...  170 us
    dot_general x64, matrix products, one_tile(): lax.dot_general(dir_cols, kernel, (((1,), (1,)), ((), ())), precision=HIG...  61.8 us
    dot_general x64, matrix products, one_tile(): lax.dot_general(dir_rows, kernel, (((1,), (0,)), ((), ())), precision=HIG...  39.9 us
    psum x1, blocking collectives, on_device(): lax.psum(gram(residual_next, residual_next), ('row', 'col'))  30.5 us
    unnamed x2, blocking collectives  30.4 us
    psum x2, blocking collectives, measure_the_slots(): incoming_x = psum(incoming_x, no)  29.1 us
    dynamic_update_slice x128, other arithmetic, add_at(): lax.dynamic_update_slice_in_dim(running, current + addend, start, axis_last)  21.8 us
  transfers between devices with their start and end apart: 4, of which 3 were waited for; matrix products, arithmetic and copies ran while one was open for 0% of the time, Pallas kernels for 0%

profile of v1, /device:TPU:0, one launch (start us, length us, event | category | flops | bytes accessed | tf_op | source)
XLA Modules:
  0.0 843.0 jit_solution(2346787852783777881)
XLA Ops:
  8.8 20.4 %all_gather.15 = f32[16,8192]{1,0:T(8,128)S(1)} all-gather(f32[16,2048]{1,0:T(8,128)S(1)} %copy-done), channel_id=1, replica_groups=mesh['groups'=2,'row'=4,'col'=4] {'col'}, dimensions={1}, use_global_device_ids=true | all-gather | bytes 655360 | tf_op jit(solution)/shard_map/all_gather | solution.py:88
  29.2 7.2 all_gather.12
  36.4 6.0 all-gather.3.cloned.1.call-done
  42.4 17.7 %all-gather.5.cloned.1.call-done = f32[32,8192]{1,0:T(8,128)} async-done(((f32[32,2048]{1,0:T(8,128)}), f32[32,8192]{1,0:T(8,128)}) %all-gather.5.cloned.1.call-update) | async-done | bytes 1048592 | tf_op jit(solution)/shard_map/all_gather | solution.py:91
  60.9 658.1 %while.22 = (s32[]{:T(128)}, f32[16,8192]{1,0:T(8,128)S(1)}, f32[8192]{0:T(1024)S(1)}, f32[16,8192]{1,0:T(8,128)S(1)}, f32[8192]{0:T(1024)S(1)}, /*index=5*/s32[...) while((s32[]{:T(128)}, f32[16,8192]{1,0:T(8,128)S(1)}, ...), condition=%wide.region_17.18_spmd, body=%wide.region_0.17_spmd.sunk | while | flops 821393472 | bytes 14518369 | solution.py:149
  88.2 2.7 fusion.150
  129.4 2.7 fusion.150
  134.0 2.7 fusion.152
  165.9 2.7 fusion.148
  170.5 2.7 fusion.150
  207.0 2.7 fusion.148
  211.6 2.7 fusion.150
  252.8 2.7 fusion.150
  293.9 2.7 fusion.150
  330.4 2.7 fusion.148
  335.0 2.7 fusion.150
  371.5 2.7 fusion.148
  376.2 2.7 fusion.150
  380.7 2.7 fusion.152
  417.3 2.7 fusion.150
  458.4 2.7 fusion.150
  540.7 2.7 fusion.150
  581.8 2.7 fusion.150
  622.9 2.7 fusion.150
  664.0 2.7 fusion.150
  705.1 2.7 fusion.150
  723.8 10.9 %all-reduce.1 = f32[8192]{0:T(1024)S(1)} all-reduce(f32[8192]{0:T(1024)S(1)} %get-tuple-element.410), channel_id=3, replica_groups=mesh['groups'=2,'row'=4,'col'=4] {'row'}, use_global_device_ids=true, to_apply=%region_19.20.clone | all-reduce | flops 8192 | bytes 65536
  734.7 19.5 %all-reduce = f32[8192]{0:T(1024)S(1)} all-reduce(f32[8192]{0:T(1024)S(1)} %get-tuple-element.409), channel_id=2, replica_groups=mesh['groups'=2,'row'=4,'col'=4] {'col'}, use_global_device_ids=true, to_apply=%region_18.19.clone | all-reduce | flops 8192 | bytes 65536
  754.3 9.7 %reduce-scatter.5.cloned.1.call-done = f32[16,2048]{1,0:T(8,128)} async-done(((f32[16,8192]{1,0:T(8,128)}), f32[16,2048]{1,0:T(8,128)}) %reduce-scatter.5.cloned.1.call-update) | async-done | bytes 131088 | tf_op jit(solution)/shard_map/reduce_scatter | solution.py:73
  765.3 18.9 %all-reduce.2 = (f32[16,16]{1,0:T(8,128)S(1)}, f32[16,16]{1,0:T(8,128)S(1)}) all-reduce(f32[16,16]{1,0:T(8,128)S(1)} %fusion.77, f32[16,16]{1,0:T(8,128)S(1)} %convolution_bitcast_fusion), channel_id=1, replica_groups=mesh['groups'=2,'row'=4,'col'=4] {'col'}, use_global_device_ids=true, to_apply=%region_26.28 | all-reduce | flops 512 | bytes 4096 | tf_op jit(solution)/shard_map/psum | solution.py:14
  784.1 10.3 %all-reduce.3 = (f32[16,16]{1,0:T(8,128)S(1)}, f32[16,16]{1,0:T(8,128)S(1)}) all-reduce(f32[16,16]{1,0:T(8,128)S(1)} %get-tuple-element.457, f32[16,16]{1,0:T(8,128)S(1)} %get-tuple-element.458), channel_id=1, replica_groups=mesh['groups'=2,'row'=4,'col'=4] {'row'}, use_global_device_ids=true, to_apply=%region_27.29 | all-reduce | flops 512 | bytes 4096 | tf_op jit(solution)/shard_map/psum | solution.py:14
  799.6 30.5 %psum.39 = f32[16,16]{1,0:T(8,128)S(1)} all-reduce(f32[16,16]{1,0:T(8,128)S(1)} %fusion.78), channel_id=1, replica_groups=mesh['groups'=2,'row'=4,'col'=4] {'row','col'}, use_global_device_ids=true, to_apply=%region_28.32 | all-reduce | flops 256 | bytes 2048 | tf_op jit(solution)/shard_map/psum | solution.py:161
  (419 shorter events, 294.6 us)
Async XLA Ops:
  7.2 35.2 %all-gather.3.cloned.1.call-start = ((), (), s32[]{:S(2)}) async-start(), calls=%async_computation.2 | async-start | bytes 1310720 | tf_op jit(solution)/shard_map/all_gather | solution.py:87
  7.9 0.9 copy-start
  7.9 52.2 %all-gather.5.cloned.1.call-start = ((), (), s32[]{:S(2)}) async-start(), calls=%async_computation.3 | async-start | bytes 1310720 | tf_op jit(solution)/shard_map/all_gather | solution.py:91
  8.7 745.7 %reduce-scatter.3.cloned.1.call-start = ((), (), s32[]{:S(2)}) async-start(), calls=%async_computation.4 | async-start | bytes 655360 | tf_op jit(solution)/shard_map/reduce_scatter | solution.py:66
  42.4 17.9 %copy-start.4 = (f32[32,8192]{1,0:T(8,128)S(1)}, f32[32,8192]{1,0:T(8,128)}, u32[]{:S(2)}) copy-start(f32[32,8192]{1,0:T(8,128)} %all-gather.3.cloned.1.call-done) | copy-start | bytes 3145732
  60.2 0.7 copy-start.8
  60.2 0.7 copy-start.9
  719.0 0.8 copy-start.2
  719.0 1.0 copy-start.1
  719.8 44.2 %reduce-scatter.5.cloned.1.call-start = ((), (), s32[]{:S(2)}) async-start(), calls=%async_computation.5 | async-start | bytes 655360 | tf_op jit(solution)/shard_map/reduce_scatter | solution.py:73
  719.9 3.7 copy-start.5
  720.4 0.7 copy-start.13
  721.1 0.7 copy-start.12
  734.7 19.6 %copy-start.11 = (f32[2048]{0:T(1024)S(1)}, f32[2048]{0:T(1024)}, u32[]{:S(2)}) copy-start(f32[2048]{0:T(1024)} %param.16) | copy-start | bytes 24580
  765.2 33.8 %copy-start.6 = (f32[16,2048]{1,0:T(8,128)S(1)}, f32[16,2048]{1,0:T(8,128)}, u32[]{:S(2)}) copy-start(f32[16,2048]{1,0:T(8,128)} %reduce-scatter.3.cloned.1.call-done) | copy-start | bytes 393220
  765.2 33.8 %copy-start.7 = (f32[16,2048]{1,0:T(8,128)S(1)}, f32[16,2048]{1,0:T(8,128)}, u32[]{:S(2)}) copy-start(f32[16,2048]{1,0:T(8,128)} %reduce-scatter.5.cloned.1.call-done) | copy-start | bytes 393220
  799.4 35.1 %copy-start.3 = (f32[16,2048]{1,0:T(8,128)}, f32[16,2048]{1,0:T(8,128)S(1)}, u32[]{:S(2)}) copy-start(f32[16,2048]{1,0:T(8,128)S(1)} %convolution_subtract_fusion) | copy-start | bytes 393220
  834.5 1.0 copy-start.10
Sparse Core Ops, SparseCore 0:
  9.6 32.7 all-gather.2
  44.0 16.1 all-gather.4
  719.9 21.7 reduce-scatter.2
  744.1 19.8 reduce-scatter.4
